TPU v7x, 256 devices: a whole 4x4x8 slice. The times are simulated.
256 devices in a mesh: grp: 4 (over z_hi, core), wide: 64 (over x, z_lo, y).
Axes of the slice: x: 4, y: 4, z: 8 (z_hi: 2, z_lo: 4; z = z_hi * 4 + z_lo), core: 2. Of those that a mesh axis runs over, the one named last changes fastest.
Arguments:
- samples: bfloat16 [4, 3072, 8, 1728], P('grp', 'wide')
- routes: int32 [4, 3072, 1], P('grp', 'wide'), may hold values from 0 to 63; in each aligned block of 48 rows (0 to 47, 48 to 95, ..., all dimensions but the last counted through in order) no two rows name the same one
- damping: float32 [64], P('wide'), may hold values from 0.25 to 4
Outputs:
- inv_root: float32 [64, 1728, 1728], P('wide', 'grp')
- scale: float32 [64], P('wide')
Inputs may be any that keep to these rules, and one draw needn't show every extreme that they name: `routes`: in the 48 strips of one device, no factor is named by more than 1 strips; every factor is named by some strip.
All inputs are finite; a program needn't handle non-finite values.
Results may differ from a plain program's by a relative error of at most 0.0037.
Values may be sent and summed in bfloat16 or wider, within the bound.
A program may use at most 64 MiB of HBM per device.

v0:
```python
import math

import jax
import jax.numpy as jnp
from jax import lax
from jax.sharding import PartitionSpec as P

POWER = 6


def per_device(samples, routes, damping):
    workers = lax.axis_size("wide")
    members = lax.axis_size("grp")
    strips = samples[0]
    slots, strip, width = strips.shape
    most = max(1, (slots + workers - 1) // workers)
    dest = routes[0, :, 0]
    onehot = (dest[:, None] == jnp.arange(workers, dtype=jnp.int32)[None, :]).astype(jnp.int32)
    rank = jnp.cumsum(onehot, 0) - onehot
    pick = onehot[:, :, None] * (
        rank[:, :, None] == jnp.arange(most, dtype=jnp.int32)[None, None, :]
    ).astype(jnp.int32)
    select = pick.reshape(slots, workers * most).T.astype(jnp.bfloat16)
    packed = jnp.dot(
        select, strips.reshape(slots, strip * width), preferred_element_type=jnp.float32
    ).astype(jnp.bfloat16)
    flags = jnp.sum(pick, 0).astype(jnp.bfloat16)
    received, got_flags = (
        lax.all_to_all(packed, "wide", split_axis=0, concat_axis=0, tiled=True),
        lax.all_to_all(flags, "wide", split_axis=0, concat_axis=0, tiled=True),
    )
    stacked = received.reshape(workers * most * strip, width)
    count = jnp.sum(got_flags.astype(jnp.float32))
    part_rows = width // members
    columns = stacked
    gram = lax.psum_scatter(
        lax.dot_general(
            columns, stacked, (((0,), (0,)), ((), ())), preferred_element_type=jnp.float32
        ),
        "grp",
        scatter_dimension=0,
        tiled=True,
    )
    offset = lax.axis_index("grp") * part_rows
    eye_rows = (
        lax.broadcasted_iota(jnp.int32, (part_rows, width), 0) + offset
        == lax.broadcasted_iota(jnp.int32, (part_rows, width), 1)
    ).astype(jnp.float32)
    total_count, trace = lax.psum((count, jnp.sum(gram * eye_rows)), "grp")
    nrows = strip * total_count
    shift = damping[0] * trace / (nrows * width)
    factor_rows = gram / nrows + shift * eye_rows
    vector = jnp.full((width,), 1.0 / math.sqrt(width), jnp.float32)
    estimate = jnp.float32(0.0)
    for turn in range(POWER):
        image_rows = jnp.dot(factor_rows, vector, precision=lax.Precision.HIGHEST)
        image = lax.all_gather(image_rows, "grp", axis=0, tiled=True)
        estimate = jnp.sum(vector * image)
        vector = image / jnp.sqrt(jnp.sum(image * image))
    bound = 1.1 * estimate
    y_first = (factor_rows / bound).astype(jnp.bfloat16)
    y_whole = lax.all_gather(y_first, "grp", axis=0, tiled=True)
    eye_whole = jnp.eye(width, dtype=jnp.float32)
    t_whole = ((3.0 * eye_whole - y_whole.astype(jnp.float32)) * 0.5).astype(jnp.bfloat16)
    t_rows = ((3.0 * eye_rows - y_first.astype(jnp.float32)) * 0.5).astype(jnp.bfloat16)
    y_second = jnp.dot(y_first, t_whole, preferred_element_type=jnp.float32).astype(jnp.bfloat16)
    columns = t_rows
    m_rows = jnp.dot(
        columns,
        lax.all_gather(y_second, "grp", axis=0, tiled=True),
        preferred_element_type=jnp.float32,
    )
    t_next = ((3.0 * eye_rows - m_rows) * 0.5).astype(jnp.bfloat16)
    result = jnp.dot(t_next, t_whole, preferred_element_type=jnp.float32)
    return (result[None], bound.reshape(1))


def solution(mesh):
    in_specs = (P("grp", "wide", None, None), P("grp", "wide", None), P("wide"))
    out_specs = (P("wide", "grp", None), P("wide"))
    return jax.shard_map(
        per_device, mesh=mesh, in_specs=in_specs, out_specs=out_specs, check_vma=False
    )
```

profile of v0, /device:TPU:1, one launch (start us, length us, event | category | flops | bytes accessed | tf_op | source)
XLA Modules:
  0.0 594.3 jit_solution(14375217176694254169)
XLA Ops:
  7.2 0.0 reduce-scatter.2.cloned.1.call-start
  7.2 0.7 fusion.16
  7.9 2.5 reshape_squeeze.3
  10.4 0.1 reduce_window_sum.13
  10.5 0.0 copy-start.1
  10.5 1.4 fusion
  11.9 0.0 copy-done.1
  11.9 0.5 broadcast.89
  12.4 2.0 reduce.3
  14.4 0.4 reshape.113
  14.9 55.6 %all_to_all.15 = bf16[64,2,6912]{2,1,0:T(2,128)(2,1)} all-to-all(bf16[64,2,6912]{2,1,0:T(2,128)(2,1)S(1)} %reshape.113), channel_id=1, replica_groups=mesh['grp'=4,'wide'=64] {'wide'}, dimensions={0} | all-to-all | bytes 3538944 | tf_op jit(solution)/shard_map/all_to_all | solution.py:29
  70.5 9.3 %reshape.114 = bf16[64,1,13824]{2,1,0:T(2,128)(2,1)S(1)} reshape(bf16[64,2,6912]{2,1,0:T(2,128)(2,1)} %all_to_all.15) | data formatting | bytes 3538944
  79.9 11.1 %reduce.2 = bf16[64,13824]{1,0:T(8,128)(2,1)} reduce(bf16[64,1,13824]{2,1,0:T(2,128)(2,1)S(1)} %reshape.114, bf16[]{:T(256)} %constant.75), dimensions={1}, to_apply=%all_to_all.11.reduce_sub_computation | reduce | bytes 3538946 | tf_op jit(solution)/shard_map/all_to_all | solution.py:29
  91.0 3.2 reshape.68
  94.3 6.4 %fusion.33 = f32[1728,1728]{1,0:T(8,128)} fusion(bf16[512,1728]{1,0:T(8,128)(2,1)S(1)} %reshape.68), kind=kOutput, calls=%fused_computation.60 | convolution fusion | flops 3057647616 | bytes 13713408 | tf_op jit(solution)/shard_map/dot_general | solution.py:37
  100.7 0.0 reduce-scatter.2.cloned.1.call-update
  100.7 0.7 copy-done.2
  101.4 0.0 copy-done.3
  101.4 0.1 select_reduce_fusion.1
  101.5 0.7 copy.6
  102.3 6.2 %all-to-all-start.1 = ((bf16[64,1,1]{2,1,0:T(2,128)(2,1)}), bf16[64,1,1]{2,1,0:T(2,128)(2,1)S(1)}, u32[]{:S(2)}, u32[]{:S(2)}) async-start(bf16[64,1,1]{2,1,0:T(2,128)(2,1)} %copy.6), calls=%async_computation.2 | async-start | bytes 65536 | tf_op jit(solution)/shard_map/all_to_all | solution.py:30
  108.5 0.0 all-gather.3.cloned.1.call-start
  109.2 0.0 copy-done.4
  109.2 0.7 dynamic-slice
  109.9 7.4 %all-to-all-done.1 = bf16[64,1,1]{2,1,0:T(2,128)(2,1)S(1)} async-done(((bf16[64,1,1]{2,1,0:T(2,128)(2,1)}), bf16[64,1,1]{2,1,0:T(2,128)(2,1)S(1)}, u32[]{:S(2)}, u32[]{:S(2)}) %all-to-all-start.1) | async-done | bytes 160 | tf_op jit(solution)/shard_map/all_to_all | solution.py:30
  117.3 0.7 convert_reduce_fusion
  118.0 160.8 %reduce-scatter.2.cloned.1.call-done = f32[432,1728]{1,0:T(8,128)} async-done(((f32[1728,1728]{1,0:T(8,128)}), f32[432,1728]{1,0:T(8,128)}) %reduce-scatter.2.cloned.1.call-update) | async-done | bytes 2986000 | tf_op jit(solution)/shard_map/reduce_scatter | solution.py:36
  278.8 3.3 select_reduce_fusion
  282.8 10.8 %all-reduce.6 = (f32[]{:T(128)}, f32[]{:T(128)}) all-reduce(f32[]{:T(128)} %select_reduce_fusion, f32[]{:T(128)} %convert_reduce_fusion), channel_id=1, replica_groups=mesh['grp'=4,'wide'=64] {'grp'}, use_global_device_ids=true, to_apply=%region_6.7 | all-reduce | flops 2 | bytes 16 | tf_op jit(solution)/shard_map/psum | solution.py:49
  295.6 2.4 select_add_fusion
  298.0 2.7 fusion.20
  300.7 0.3 dynamic-update-slice
  300.9 9.7 %all-reduce = f32[1728]{0:T(1024)S(1)} all-reduce(f32[1728]{0:T(1024)S(1)} %dynamic-update-slice), channel_id=1, replica_groups=mesh['grp'=4,'wide'=64] {'grp'}, use_global_device_ids=true, to_apply=%add | all-reduce | flops 1728 | bytes 13824
  310.6 0.6 multiply_reduce_fusion.5
  311.9 2.7 fusion.34
  314.6 0.3 dynamic-update-slice.1
  314.9 9.8 %all-reduce.1 = f32[1728]{0:T(1024)S(1)} all-reduce(f32[1728]{0:T(1024)S(1)} %dynamic-update-slice.1), channel_id=1, replica_groups=mesh['grp'=4,'wide'=64] {'grp'}, use_global_device_ids=true, to_apply=%add.1 | all-reduce | flops 1728 | bytes 13824
  324.6 0.6 multiply_reduce_fusion.4
  325.9 2.7 fusion.35
  328.6 0.3 dynamic-update-slice.2
  328.8 14.5 %all-reduce.2 = f32[1728]{0:T(1024)S(1)} all-reduce(f32[1728]{0:T(1024)S(1)} %dynamic-update-slice.2), channel_id=1, replica_groups=mesh['grp'=4,'wide'=64] {'grp'}, use_global_device_ids=true, to_apply=%add.2 | all-reduce | flops 1728 | bytes 13824
  343.3 0.6 multiply_reduce_fusion.3
  344.6 2.7 fusion.36
  347.3 0.3 dynamic-update-slice.3
  347.6 9.9 %all-reduce.3 = f32[1728]{0:T(1024)S(1)} all-reduce(f32[1728]{0:T(1024)S(1)} %dynamic-update-slice.3), channel_id=1, replica_groups=mesh['grp'=4,'wide'=64] {'grp'}, use_global_device_ids=true, to_apply=%add.3 | all-reduce | flops 1728 | bytes 13824
  357.5 0.6 multiply_reduce_fusion.2
  358.8 2.7 fusion.37
  361.5 0.3 dynamic-update-slice.4
  361.7 10.1 %all-reduce.4 = f32[1728]{0:T(1024)S(1)} all-reduce(f32[1728]{0:T(1024)S(1)} %dynamic-update-slice.4), channel_id=1, replica_groups=mesh['grp'=4,'wide'=64] {'grp'}, use_global_device_ids=true, to_apply=%add.4 | all-reduce | flops 1728 | bytes 13824
  371.8 0.6 multiply_reduce_fusion.1
  373.2 2.7 fusion.38
  375.8 0.3 dynamic-update-slice.5
  376.1 9.7 %all-reduce.5 = f32[1728]{0:T(1024)S(1)} all-reduce(f32[1728]{0:T(1024)S(1)} %dynamic-update-slice.5), channel_id=1, replica_groups=mesh['grp'=4,'wide'=64] {'grp'}, use_global_device_ids=true, to_apply=%add.5 | all-reduce | flops 1728 | bytes 13824
  385.8 0.6 multiply_reduce_fusion
  387.1 3.7 divide_convert_fusion
  390.8 0.0 all-gather.3.cloned.1.call-update
  390.8 0.0 copy-start
  390.8 0.3 all-gather.5.cloned.1.call-start
  391.1 90.4 %all-gather.3.cloned.1.call-done = bf16[1728,1728]{1,0:T(8,128)(2,1)} async-done(((bf16[432,1728]{1,0:T(8,128)(2,1)}), bf16[1728,1728]{1,0:T(8,128)(2,1)}) %all-gather.3.cloned.1.call-update) | async-done | bytes 5971984 | tf_op jit(solution)/shard_map/all_gather | solution.py:62
  481.5 7.5 %fusion.8 = bf16[432,1728]{1,0:T(8,128)(2,1)} fusion(bf16[432,1728]{1,0:T(8,128)(2,1)} %divide_convert_fusion, bf16[1728,1728]{1,0:T(8,128)(2,1)} %all-gather.3.cloned.1.call-done), kind=kOutput, calls=%fused_computation.17 | convolution fusion | flops 2598552576 | bytes 8957952 | tf_op jit(solution)/shard_map/dot_general | solution.py:66
  489.0 0.0 all-gather.5.cloned.1.call-update
  489.0 85.2 %all-gather.5.cloned.1.call-done = bf16[1728,1728]{1,0:T(8,128)(2,1)} async-done(((bf16[432,1728]{1,0:T(8,128)(2,1)}), bf16[1728,1728]{1,0:T(8,128)(2,1)}) %all-gather.5.cloned.1.call-update) | async-done | bytes 5971984 | tf_op jit(solution)/shard_map/all_gather | solution.py:70
  574.2 0.0 copy-done
  574.2 12.3 %fusion.7 = f32[1,432,1728]{2,1,0:T(8,128)} fusion(bf16[1728,1728]{1,0:T(8,128)(2,1)} %all-gather.3.cloned.1.call-done, bf16[1728,1728]{1,0:T(8,128)(2,1)} %all-gather.5.cloned.1.call-done, bf16[432,1728]{1,0:T(8,128)(2,1)S(1)} %copy-done, s32[432]{0:T(512)S(1)} %iota_add_fusion), kind=kOutput, calls=%fused_computation.16 | convolution fusion | flops 5185907712 | bytes 16424640 | tf_op jit(solution)/shard_map/dot_general | solution.py:74
  (21 shorter events, 0.1 us)
Async XLA Ops:
  7.2 271.7 %reduce-scatter.2.cloned.1.call-start = ((), (), s32[]{:S(2)}) async-start(), calls=%async_computation.3 | async-start | bytes 15482880 | tf_op jit(solution)/shard_map/reduce_scatter | solution.py:36
  10.5 1.4 copy-start.1
  100.7 0.7 copy-start.2
  100.7 0.7 copy-start.3
  100.7 8.6 %copy-start.4 = (u32[256]{0:T(256)S(1)}, u32[256]{0:T(256)}, u32[]{:S(2)}) copy-start(u32[256]{0:T(256)} %constant.41) | copy-start | bytes 3076
  102.3 15.1 %all-to-all-start.1 = ((bf16[64,1,1]{2,1,0:T(2,128)(2,1)}), bf16[64,1,1]{2,1,0:T(2,128)(2,1)S(1)}, u32[]{:S(2)}, u32[]{:S(2)}) async-start(bf16[64,1,1]{2,1,0:T(2,128)(2,1)} %copy.6), calls=%async_computation.2 | async-start | bytes 65536 | tf_op jit(solution)/shard_map/all_to_all | solution.py:30
  108.5 373.0 %all-gather.3.cloned.1.call-start = ((), (), s32[]{:S(2)}) async-start(), calls=%async_computation.4 | async-start | bytes 7741440 | tf_op jit(solution)/shard_map/all_gather | solution.py:62
  390.8 183.4 %copy-start = (bf16[432,1728]{1,0:T(8,128)(2,1)S(1)}, bf16[432,1728]{1,0:T(8,128)(2,1)}, u32[]{:S(2)}) copy-start(bf16[432,1728]{1,0:T(8,128)(2,1)} %divide_convert_fusion) | copy-start | bytes 4478980
  390.8 183.3 %all-gather.5.cloned.1.call-start = ((), (), s32[]{:S(2)}) async-start(), calls=%async_computation.5 | async-start | bytes 7741440 | tf_op jit(solution)/shard_map/all_gather | solution.py:70
Sparse Core Ops, SparseCore 0:
  100.8 177.9 reduce-scatter.1
  390.9 90.4 all-gather.2
  489.1 85.0 all-gather.4
where the time goes:
time: 603 us; the launch traced here: 594 us
  waiting for transfers between devices  344 us (57%)
  blocking collectives  130 us (22%)
  matrix products  43.5 us (7%)
  other arithmetic  27.8 us (5%)
  between operations  22.7 us (4%)
  local copies, waits for them, and re-layouts  19.7 us (3%)
  starting transfers between devices  6.57 us (1%)
    reduce_scatter x1, waiting for transfers between devices, per_device(): lax.psum_scatter(lax.dot_general(columns, stacked, (((0,), (0,)), ((), ()...  161 us
    all_gather x1, waiting for transfers between devices, per_device(): y_whole = lax.all_gather(y_first, 'grp', axis=0, tiled=True)  90.4 us
    all_gather x1, waiting for transfers between devices, per_device(): lax.all_gather(y_second, 'grp', axis=0, tiled=True)  85.2 us
    unnamed x6, blocking collectives  63.7 us
    all_to_all x1, blocking collectives, per_device(): lax.all_to_all(packed, 'wide', split_axis=0, concat_axis=0, tiled=True)  55.6 us
    dot_general x6, matrix products, per_device(): image_rows = jnp.dot(factor_rows, vector, precision=lax.Precision.HIGHEST)  15.9 us
    all_to_all x2, other arithmetic, per_device(): lax.all_to_all(packed, 'wide', split_axis=0, concat_axis=0, tiled=True)  13.1 us
    unnamed x25, local copies, waits for them, and re-layouts  12.7 us
  transfers between devices with their start and end apart: 4, of which 4 were waited for; matrix products, arithmetic and copies ran while one was open for 0% of the time, Pallas kernels for 0%

commit v1 on v0

v1 whole, which is shorter than its diff:
```python
import functools
import math

import jax
import jax.numpy as jnp
from jax import lax
from jax.experimental import pallas as pl
from jax.experimental.pallas import tpu as pltpu
from jax.sharding import PartitionSpec as P

POWER = 6
MESH = pl.DeviceIdType.MESH
F32, BF16 = jnp.float32, jnp.bfloat16
LANES = 128
TILE = 256

STEPS = (
    (0, 0), (1, 0), (1, 1), (3, 0), (3, 3), (0, 1), (1, 3), (0, 3),
    (3, 1), (2, 1), (2, 0), (1, 2), (0, 2), (2, 3), (2, 2), (3, 2),
)
LAG = 6


def device(z, core, x, y):
    return (lax.div(z, 4) * 2 + core, x * 16 + lax.rem(z, 4) * 4 + y)


def fused(width, strip, ext, routes, damping, out, scale, sib_out, sib_in, own, cells, staged, stack, gram, y_all, t_all, t_rows, a_rows, t_next, column, sib_send, sib_recv, plane_send, plane_recv, z_send, group_recv, pass_send, pass_recv):
    member, worker = lax.axis_index("grp"), lax.axis_index("wide")
    core = lax.rem(member, 2)
    x, y = lax.div(worker, 16), lax.rem(worker, 4)
    z = lax.div(member, 2) * 4 + lax.rem(lax.div(worker, 4), 4)
    place = x * 4 + y
    even = lax.rem(z, 2) == core
    wide = ext.shape[1]
    tiles = wide // TILE
    rows = out.shape[0]
    pair_rows = 2 * strip

    def peer(dx, dy):
        return lax.rem(x + dx, 4), lax.rem(y + dy, 4)

    barrier = pltpu.get_barrier_semaphore()
    pl.semaphore_signal(barrier, inc=1, device_id=device(z, 1 - core, x, y), device_id_type=MESH)
    for dx, dy in STEPS[1:]:
        px, py = peer(dx, dy)
        pl.semaphore_signal(barrier, inc=1, device_id=device(z, core, px, py), device_id_type=MESH)
    for dz in range(1, 8):
        pl.semaphore_signal(barrier, inc=1, device_id=device(lax.rem(z + dz, 8), lax.rem(z, 2), x, y), device_id_type=MESH)

    def choose(parity):
        shape = (16 * pair_rows, ext.shape[0])
        row = lax.broadcasted_iota(jnp.int32, shape, 0)
        col = lax.broadcasted_iota(jnp.int32, shape, 1)
        where = row // pair_rows
        plane = 2 * ((row // strip) % 2) + parity
        factor = (where // 4) * 16 + plane * 4 + where % 4
        hit = (routes[...] == factor) & (row % strip == col % strip)
        pick = jnp.where(hit, 1.0, 0.0).astype(BF16)
        chosen = jnp.dot(pick, ext[...], preferred_element_type=F32)
        return chosen.astype(BF16).reshape(16, pair_rows, wide)

    sib_out[...] = choose(1 - core)
    pl.semaphore_wait(barrier, jnp.where(even, 22, 24))
    sibling = device(z, 1 - core, x, y)

    def sib_copy(step):
        px, py = peer(*STEPS[step])
        at = px * 4 + py
        return pltpu.make_async_remote_copy(
            sib_out.at[at], sib_in.at[at], sib_send.at[step], sib_recv.at[step], device_id=sibling, device_id_type=MESH
        )

    for step in range(16):
        sib_copy(step).start()
    own[...] = choose(core)

    def plane_copy(step):
        px, py = peer(*STEPS[step])
        return pltpu.make_async_remote_copy(
            cells.at[pl.ds(2 * (px * 4 + py), 2)],
            staged.at[pl.ds(2 * place, 2)],
            plane_send.at[step],
            plane_recv.at[step],
            device_id=device(z, core, px, py),
            device_id_type=MESH,
        )

    for step in range(16):
        px, py = peer(*STEPS[step])
        at = px * 4 + py
        sib_copy(step).wait_recv()
        mine, other = own[at].astype(F32), sib_in[at].astype(F32)
        for j in range(2):
            part = slice(j * strip, (j + 1) * strip)
            cells[2 * at + j] = jnp.concatenate([mine[part], other[part]], 0).astype(BF16)
        if step > 0:
            plane_copy(step).start()

    def origin(step):
        dx, dy = STEPS[step]
        return peer(4 - dx, 4 - dy)

    def z_copy(step, dz, slot, near=False):
        sx, sy = origin(step)
        target = lax.rem(z + dz, 8)
        j = lax.div(lax.rem(target, 4), 2)
        source = cells if step == 0 else staged
        cell = source.at[2 * (sx * 4 + sy) + j]
        landing = stack.at[step * 8 + z]
        if near:
            return pltpu.make_async_copy(cell, landing, group_recv.at[step])
        return pltpu.make_async_remote_copy(
            cell,
            landing,
            z_send.at[step, slot],
            group_recv.at[step],
            device_id=device(target, lax.rem(sx + sy, 2), x, y),
            device_id_type=MESH,
        )

    def direct(step):
        sx, sy = origin(step)
        return lax.rem(sx + sy, 2) == core

    def z_start(step):
        if step > 0:
            plane_copy(step).wait_recv()

        @pl.when(even)
        def _():
            for slot, dz in enumerate((4, 2, 6)):
                z_copy(step, dz, slot).start()

            @pl.when(direct(step))
            def _():
                z_copy(step, 0, 3, near=True).start()

            @pl.when(jnp.logical_not(direct(step)))
            def _():
                z_copy(step, 0, 3).start()

        @pl.when(jnp.logical_not(even))
        def _():
            for slot, dz in enumerate((5, 3, 1, 7)):
                z_copy(step, dz, slot).start()

    def z_finish(step):
        for slot in range(3):
            z_copy(step, 1, slot).wait_send()

        @pl.when(jnp.logical_not(even & direct(step)))
        def _():
            z_copy(step, 1, 3).wait_send()

    def pass_copy(step):
        group = stack.at[pl.ds(step * 8, 8)]
        return pltpu.make_async_remote_copy(
            group, group, pass_send.at[step], pass_recv.at[step], device_id=sibling, device_id_type=MESH
        )

    def arrive(pair):
        for step in (2 * pair, 2 * pair + 1):
            group = stack.at[pl.ds(step * 8, 8)]

            @pl.when(direct(step))
            def _():
                pltpu.make_async_copy(group, group, group_recv.at[step]).wait()
                pass_copy(step).start()

        for step in (2 * pair, 2 * pair + 1):

            @pl.when(jnp.logical_not(direct(step)))
            def _():
                pass_copy(step).wait_recv()

    depth = 16 * pair_rows

    def accumulate(pair):
        block = stack[pl.ds(pair * 16, 16)].reshape(depth, wide)

        def body(i, _):
            left = stack[pl.ds(pair * 16, 16), :, pl.ds(pl.multiple_of(i * TILE, TILE), TILE)].reshape(depth, TILE)
            term = lax.dot_general(left, block, (((0,), (0,)), ((), ())), preferred_element_type=F32)
            at = pl.ds(pl.multiple_of(i * TILE, TILE), TILE)
            if pair == 0:
                gram[at, :] = term
            else:
                gram[at, :] += term
            return 0

        lax.fori_loop(0, tiles, body, 0)

    for turn in range(8 + LAG // 2):
        if turn < 8:
            z_start(2 * turn)
            z_start(2 * turn + 1)
        if turn >= LAG // 2:
            arrive(turn - LAG // 2)
            accumulate(turn - LAG // 2)

    eye = (
        lax.broadcasted_iota(jnp.int32, (LANES, LANES), 0) == lax.broadcasted_iota(jnp.int32, (LANES, LANES), 1)
    ).astype(F32)
    last = wide - LANES
    inside = lax.broadcasted_iota(jnp.int32, (1, LANES), 1) < width - last
    lane = lax.broadcasted_iota(jnp.int32, (1, LANES), 1)
    count = jnp.sum(jnp.where(lane == width - last, gram[pl.ds(width, 8), pl.ds(last, LANES)][0:1], 0.0))

    def clear(i, _):
        at = pl.ds(pl.multiple_of(i * TILE, TILE), TILE)
        gram[at, pl.ds(last, LANES)] = jnp.where(inside, gram[at, pl.ds(last, LANES)], 0.0)
        return 0

    lax.fori_loop(0, tiles, clear, 0)
    gram[pl.ds(width, wide - width), :] = jnp.zeros((wide - width, wide), F32)
    diagonal = jnp.zeros((LANES, LANES), F32)
    for b in range(wide // LANES):
        diagonal += gram[b * LANES : (b + 1) * LANES, b * LANES : (b + 1) * LANES] * eye
    trace = jnp.sum(diagonal)
    lift = damping[0] * trace / width
    unit = width / trace
    for b in range(wide // LANES):
        at = slice(b * LANES, (b + 1) * LANES)
        gram[at, at] += lift * (eye if b < wide // LANES - 1 else jnp.where(inside, eye, 0.0))

    chunk = 64

    def to_column(row, factor):
        def body(i, _):
            at = pl.ds(pl.multiple_of(i * chunk, chunk), chunk)
            total = jnp.sum(gram[at, :] * row, axis=1, keepdims=True) * factor
            column[at, :] = jnp.broadcast_to(total, (chunk, LANES))
            return 0

        lax.fori_loop(0, wide // chunk, body, 0)

    def to_row(factor):
        def body(i, sums):
            at = pl.ds(pl.multiple_of(i * chunk, chunk), chunk)
            value = column[at, :]
            return tuple(
                part + jnp.sum((gram[at, b * LANES : (b + 1) * LANES] * value).reshape(chunk // 8, 8, LANES), axis=0)
                for b, part in enumerate(sums)
            )

        sums = lax.fori_loop(0, wide // chunk, body, tuple(jnp.zeros((8, LANES), F32) for _ in range(wide // LANES)))
        return jnp.concatenate([jnp.sum(part, axis=0, keepdims=True) for part in sums], axis=1) * factor

    lane_all = lax.broadcasted_iota(jnp.int32, (1, wide), 1)
    vector = jnp.where(lane_all < width, 1.0 / math.sqrt(width), 0.0).astype(F32)
    to_column(vector, unit)
    vector = to_row(unit)
    to_column(vector, unit)
    norm = jnp.sum(column[...] * column[...]) * (1.0 / LANES)
    vector = to_row(unit * lax.rsqrt(norm))
    to_column(vector, unit)
    fifth = jnp.concatenate(
        [jnp.sum(column[b * LANES : (b + 1) * LANES, :] * eye, axis=0, keepdims=True) for b in range(wide // LANES)], axis=1
    )
    sixth = to_row(unit)
    bound = 1.1 * (jnp.sum(fifth * sixth) / jnp.sum(fifth * fifth))
    scale[0, 0] = bound * (trace / (count * width))
    rate = unit / bound

    def normalize(i, _):
        at = pl.ds(pl.multiple_of(i * LANES, LANES), LANES)
        y_part = (gram[at, :] * rate).astype(BF16)
        row = lax.broadcasted_iota(jnp.int32, (LANES, wide), 0) + i * LANES
        col = lax.broadcasted_iota(jnp.int32, (LANES, wide), 1)
        three = jnp.where((row == col) & (col < width), 3.0, 0.0)
        y_all[at, :] = y_part
        t_all[at, :] = ((three - y_part.astype(F32)) * 0.5).astype(BF16)
        return 0

    lax.fori_loop(0, wide // LANES, normalize, 0)

    first = member * rows
    t_rows[...] = t_all[pl.ds(pl.multiple_of(first, 16), rows), :]

    def step_one(i, _):
        at = pl.ds(pl.multiple_of(i * TILE, TILE), TILE)
        a_rows[:, at] = jnp.dot(t_rows[...], y_all[:, at], preferred_element_type=F32).astype(BF16)
        return 0

    lax.fori_loop(0, tiles, step_one, 0)

    def step_two(i, _):
        at = pl.ds(pl.multiple_of(i * TILE, TILE), TILE)
        m_part = jnp.dot(a_rows[...], t_all[:, at], preferred_element_type=F32)
        row = lax.broadcasted_iota(jnp.int32, (rows, TILE), 0) + first
        col = lax.broadcasted_iota(jnp.int32, (rows, TILE), 1) + i * TILE
        three = jnp.where(row == col, 3.0, 0.0)
        t_next[:, at] = ((three - m_part) * 0.5).astype(BF16)
        return 0

    lax.fori_loop(0, tiles, step_two, 0)

    def step_three(i, _):
        at = pl.ds(pl.multiple_of(i * TILE, TILE), TILE)
        out[:, at] = jnp.dot(t_next[...], t_all[:, at], preferred_element_type=F32)
        return 0

    lax.fori_loop(0, tiles - 1, step_three, 0)
    tail = (tiles - 1) * TILE
    out[:, tail:width] = jnp.dot(t_next[...], t_all[:, tail:], preferred_element_type=F32)[:, : width - tail]

    for step in range(16):
        sib_copy(step).wait_send()
        if step > 0:
            plane_copy(step).wait_send()
        z_finish(step)

        @pl.when(direct(step))
        def _():
            pass_copy(step).wait_send()


def per_device(samples, routes, damping):
    members = lax.axis_size("grp")
    _, slots, strip, width = samples.shape
    wide = -(-width // TILE) * TILE
    rows = width // members
    strips = samples[0].reshape(slots * strip, width)
    mark = (lax.broadcasted_iota(jnp.int32, (slots * strip, wide - width), 1) == 0).astype(BF16)
    ext = jnp.concatenate([strips, mark], axis=1)
    named = jnp.repeat(routes[0, :, 0], strip)[None]
    vmem = pl.BlockSpec(memory_space=pltpu.VMEM)
    smem = pl.BlockSpec(memory_space=pltpu.SMEM)
    dma = pltpu.SemaphoreType.DMA
    result, scale = pl.pallas_call(
        functools.partial(fused, width, strip),
        out_shape=(jax.ShapeDtypeStruct((rows, width), F32), jax.ShapeDtypeStruct((1, 1), F32)),
        in_specs=[vmem, vmem, smem],
        out_specs=(vmem, smem),
        scratch_shapes=[
            pltpu.VMEM((16, 2 * strip, wide), BF16),
            pltpu.VMEM((16, 2 * strip, wide), BF16),
            pltpu.VMEM((16, 2 * strip, wide), BF16),
            pltpu.VMEM((32, 2 * strip, wide), BF16),
            pltpu.VMEM((32, 2 * strip, wide), BF16),
            pltpu.VMEM((128, 2 * strip, wide), BF16),
            pltpu.VMEM((wide, wide), F32),
            pltpu.VMEM((wide, wide), BF16),
            pltpu.VMEM((wide, wide), BF16),
            pltpu.VMEM((rows, wide), BF16),
            pltpu.VMEM((rows, wide), BF16),
            pltpu.VMEM((rows, wide), BF16),
            pltpu.VMEM((wide, LANES), F32),
            dma((16,)),
            dma((16,)),
            dma((16,)),
            dma((16,)),
            dma((16, 4)),
            dma((16,)),
            dma((16,)),
            dma((16,)),
        ],
        compiler_params=pltpu.CompilerParams(
            collective_id=0, has_side_effects=True, vmem_limit_bytes=60 * 1024 * 1024
        ),
        name="inverse_root",
    )(ext, named, damping)
    return (result[None], scale.reshape(1))


def solution(mesh):
    in_specs = (P("grp", "wide", None, None), P("grp", "wide", None), P("wide"))
    out_specs = (P("wide", "grp", None), P("wide"))
    return jax.shard_map(
        per_device, mesh=mesh, in_specs=in_specs, out_specs=out_specs, check_vma=False
    )
```

time: 603 us -> 144 us (0.24); the launches traced: 594 us -> 143 us
  waiting for transfers between devices: 344 us -> 0 us
  Pallas kernels: 0 us -> 132 us
  blocking collectives: 130 us -> 0 us
  matrix products: 43.5 us -> 0 us
  other arithmetic: 27.8 us -> 2.65 us
  between operations: 22.7 us -> 3.11 us
  local copies, waits for them, and re-layouts: 19.7 us -> 5.21 us
  starting transfers between devices: 6.57 us -> 0 us
    all_gather x2 -> x0, waiting for transfers between devices: 176 us -> none  [the longest x1 90.4 us: per_device(): y_whole = lax.all_gather(y_first, 'grp', axis=0, tiled=True)]
    reduce_scatter x1 -> x0, waiting for transfers between devices: 161 us -> none  [per_device(): lax.psum_scatter(lax.dot_general(columns, stacked, (((0,), (0,)), ((), ()...]
    pallas_call x0 -> x1, Pallas kernels: none -> 132 us  [per_device(): pl.pallas_call(functools.partial(fused, width, strip), out_shape=(jax.Sha...]
    unnamed x6 -> x0, blocking collectives: 63.7 us -> none
    all_to_all x1 -> x0, blocking collectives: 55.6 us -> none  [per_device(): lax.all_to_all(packed, 'wide', split_axis=0, concat_axis=0, tiled=True)]
    dot_general x10 -> x0, matrix products: 43.5 us -> none  [the longest x6 15.9 us: per_device(): image_rows = jnp.dot(factor_rows, vector, precision=lax.Precision.HIGHEST)]
    all_to_all x2 -> x0, other arithmetic: 13.1 us -> none  [per_device(): lax.all_to_all(packed, 'wide', split_axis=0, concat_axis=0, tiled=True)]
    psum x1 -> x0, blocking collectives: 10.8 us -> none  [per_device(): total_count, trace = lax.psum((count, jnp.sum(gram * eye_rows)), 'grp')]
  transfers between devices with their start and end apart: 4 -> 0, of which waited for: 4 -> 0; matrix products, arithmetic and copies ran while one was open for 0% -> 0% of each run, Pallas kernels for 0% -> 0%
where the time goes in v1:
time: 144 us; the launch traced here: 143 us
  Pallas kernels  132 us (92%)
  local copies, waits for them, and re-layouts  5.21 us (4%)
  between operations  3.11 us (2%)
  other arithmetic  2.65 us (2%)
    pallas_call x1, Pallas kernels, per_device(): pl.pallas_call(functools.partial(fused, width, strip), out_shape=(jax.Sha...  132 us
    unnamed x1, local copies, waits for them, and re-layouts  3.72 us

profile of v1, /device:TPU:1, one launch (start us, length us, event | category | flops | bytes accessed | tf_op | source)
XLA Modules:
  0.0 143.4 jit_solution(4671850077159139936)
XLA Ops:
  1.3 0.1 pad.1.clone
  1.4 0.7 broadcast_in_dim.6
  2.1 0.7 broadcast_in_dim_reshape.3.routes
  2.8 2.6 %pad_maximum_fusion.ext = bf16[384,1792]{1,0:T(8,128)(2,1)} fusion(bf16[384,1728]{1,0:T(8,128)(2,1)} %bitcast.5, bf16[1792]{0:T(1024)(128)(2,1)S(1)} %pad.1.clone), kind=kLoop, calls=%fused_computation | loop fusion | flops 2752512 | bytes 2706944 | tf_op jit(solution)/shard_map/concatenate | solution.py:326
  5.4 132.5 %inverse_root.1 = (f32[432,1728]{1,0:T(8,128)}, f32[1,1]{1,0:T(1,128)}) custom-call(bf16[384,1792]{1,0:T(8,128)(2,1)} %pad_maximum_fusion.ext, s32[1,384]{1,0:T(1,128)} %broadcast_in_dim_reshape.3.routes, f32[1]{0:T(128)S(6)} %copy.7.damping), custom_call_target="tpu_custom_call" | custom-call | tf_op jit(solution)/shard_map/inverse_root/pallas_call | solution.py:331
  137.9 3.7 %copy.8 = f32[1,432,1728]{2,1,0:T(8,128)} copy(f32[1,432,1728]{2,1,0:T(8,128)} %bitcast.4) | data formatting | bytes 5971968
  (1 shorter events, 0.0 us)

commit v2 on v1

v2 whole, which is shorter than its diff:
```python
import functools
import math

import jax
import jax.numpy as jnp
from jax import lax
from jax.experimental import pallas as pl
from jax.experimental.pallas import tpu as pltpu
from jax.sharding import PartitionSpec as P

POWER = 6
MESH = pl.DeviceIdType.MESH
F32, BF16 = jnp.float32, jnp.bfloat16
LANES = 128
TILE = 256

STEPS = (
    (0, 0), (1, 0), (1, 1), (3, 0), (3, 3), (0, 1), (1, 3), (0, 3),
    (3, 1), (2, 1), (2, 0), (1, 2), (0, 2), (2, 3), (2, 2), (3, 2),
)
LAG = 6


def device(z, core, x, y):
    return (lax.div(z, 4) * 2 + core, x * 16 + lax.rem(z, 4) * 4 + y)


def fused(width, strip, slots, strips, routes, damping, out, scale, ext, chosen, staged, cells, stack, gram, t_all, t_rows, a_rows, t_next, vectors, plane_send, plane_recv, z_send, group_recv, pass_send, pass_recv):
    member, worker = lax.axis_index("grp"), lax.axis_index("wide")
    core = lax.rem(member, 2)
    x, y = lax.div(worker, 16), lax.rem(worker, 4)
    z = lax.div(member, 2) * 4 + lax.rem(lax.div(worker, 4), 4)
    even = lax.rem(z, 2) == core
    wide = ext.shape[1]
    tiles = wide // TILE
    rows = out.shape[0]
    pair_rows = 2 * strip
    last = wide - LANES

    def peer(dx, dy):
        return lax.rem(x + dx, 4), lax.rem(y + dy, 4)

    barrier = pltpu.get_barrier_semaphore()
    pl.semaphore_signal(barrier, inc=1, device_id=device(z, 1 - core, x, y), device_id_type=MESH)
    for dx, dy in STEPS[1:]:
        px, py = peer(dx, dy)
        for there in range(2):
            pl.semaphore_signal(barrier, inc=1, device_id=device(z, there, px, py), device_id_type=MESH)
    for dz in range(1, 8):
        pl.semaphore_signal(barrier, inc=1, device_id=device(lax.rem(z + dz, 8), lax.rem(z, 2), x, y), device_id_type=MESH)

    ext[:, :last] = strips[:, :last]
    mark = lax.broadcasted_iota(jnp.int32, (slots * strip, wide - width), 1) == 0
    ext[:, last:] = jnp.concatenate([strips[:, last:].astype(F32), jnp.where(mark, 1.0, 0.0)], axis=1).astype(BF16)
    spread = lax.broadcasted_iota(jnp.int32, (slots, slots * strip), 1) // strip == lax.broadcasted_iota(
        jnp.int32, (slots, slots * strip), 0
    )
    named = jnp.broadcast_to(routes[...].astype(F32), (8, slots)).astype(BF16)
    named = jnp.dot(named, jnp.where(spread, 1.0, 0.0).astype(BF16), preferred_element_type=F32)[0:1].astype(jnp.int32)
    shape = (32 * pair_rows, slots * strip)
    row = lax.broadcasted_iota(jnp.int32, shape, 0)
    col = lax.broadcasted_iota(jnp.int32, shape, 1)
    place, plane = row // (2 * pair_rows), 2 * ((row // strip) % 2) + (row // pair_rows) % 2
    factor = (place // 4) * 16 + plane * 4 + place % 4
    pick = jnp.where((named == factor) & (row % strip == col % strip), 1.0, 0.0).astype(BF16)
    chosen[...] = jnp.dot(pick, ext[...], preferred_element_type=F32).astype(BF16).reshape(32, pair_rows, wide)
    pl.semaphore_wait(barrier, jnp.where(even, 37, 39))

    def plane_copy(step, there):
        px, py = peer(*STEPS[step])
        return pltpu.make_async_remote_copy(
            chosen.at[2 * (px * 4 + py) + there],
            staged.at[2 * step + core],
            plane_send.at[step, there],
            plane_recv.at[step, core],
            device_id=device(z, there, px, py),
            device_id_type=MESH,
        )

    def plane_each(step, act):
        for there in range(2):
            if step > 0:
                act(plane_copy(step, there))
            else:

                @pl.when(core != there)
                def _():
                    act(plane_copy(step, there))

    def plane_wait(step):
        for source in range(2):
            landed = staged.at[2 * step + source]
            if step > 0:
                pltpu.make_async_copy(landed, landed, plane_recv.at[step, source]).wait()
            else:

                @pl.when(core != source)
                def _():
                    pltpu.make_async_copy(landed, landed, plane_recv.at[step, source]).wait()

    for step in range(16):
        plane_each(step, lambda copy: copy.start())
    staged[core] = chosen[2 * (x * 4 + y) + core]

    def origin(step):
        dx, dy = STEPS[step]
        return peer(4 - dx, 4 - dy)

    def direct(step):
        sx, sy = origin(step)
        return lax.rem(sx + sy, 2) == core

    def z_copy(step, dz, slot, near=False):
        sx, sy = origin(step)
        target = lax.rem(z + dz, 8)
        cell = cells.at[2 * step + lax.div(lax.rem(target, 4), 2)]
        landing = stack.at[step * 8 + z]
        if near:
            return pltpu.make_async_copy(cell, landing, group_recv.at[step])
        return pltpu.make_async_remote_copy(
            cell,
            landing,
            z_send.at[step, slot],
            group_recv.at[step],
            device_id=device(target, lax.rem(sx + sy, 2), x, y),
            device_id_type=MESH,
        )

    def z_start(step):
        plane_wait(step)
        one, two = staged[2 * step].astype(F32), staged[2 * step + 1].astype(F32)
        for j in range(2):
            part = slice(j * strip, (j + 1) * strip)
            cells[2 * step + j] = jnp.concatenate([one[part], two[part]], 0).astype(BF16)

        @pl.when(even)
        def _():
            for slot, dz in enumerate((4, 2, 6)):
                z_copy(step, dz, slot).start()

            @pl.when(direct(step))
            def _():
                z_copy(step, 0, 3, near=True).start()

            @pl.when(jnp.logical_not(direct(step)))
            def _():
                z_copy(step, 0, 3).start()

        @pl.when(jnp.logical_not(even))
        def _():
            for slot, dz in enumerate((5, 3, 1, 7)):
                z_copy(step, dz, slot).start()

    def z_finish(step):
        for slot in range(3):
            z_copy(step, 1, slot).wait_send()

        @pl.when(jnp.logical_not(even & direct(step)))
        def _():
            z_copy(step, 1, 3).wait_send()

    sibling = device(z, 1 - core, x, y)

    def pass_copy(step):
        group = stack.at[pl.ds(step * 8, 8)]
        return pltpu.make_async_remote_copy(
            group, group, pass_send.at[step], pass_recv.at[step], device_id=sibling, device_id_type=MESH
        )

    def arrive(pair):
        for step in (2 * pair, 2 * pair + 1):
            group = stack.at[pl.ds(step * 8, 8)]

            @pl.when(direct(step))
            def _():
                pltpu.make_async_copy(group, group, group_recv.at[step]).wait()
                pass_copy(step).start()

        for step in (2 * pair, 2 * pair + 1):

            @pl.when(jnp.logical_not(direct(step)))
            def _():
                pass_copy(step).wait_recv()

    depth, half = 16 * pair_rows, wide // 2

    def accumulate(pair):
        def body(i, _):
            at = pl.ds(pl.multiple_of(i * half, LANES), half)
            left = stack[pl.ds(pair * 16, 16), :, at].reshape(depth, half)
            block = stack[pl.ds(pair * 16, 16)].reshape(depth, wide)
            term = lax.dot_general(left, block, (((0,), (0,)), ((), ())), preferred_element_type=F32)
            if pair == 0:
                gram[at, :] = term
            else:
                gram[at, :] += term
            return 0

        lax.fori_loop(0, 2, body, 0)

    for turn in range(8 + LAG // 2):
        if turn < 8:
            z_start(2 * turn)
            z_start(2 * turn + 1)
        if turn >= LAG // 2:
            arrive(turn - LAG // 2)
            accumulate(turn - LAG // 2)

    eye = (
        lax.broadcasted_iota(jnp.int32, (LANES, LANES), 0) == lax.broadcasted_iota(jnp.int32, (LANES, LANES), 1)
    ).astype(F32)
    inside = lax.broadcasted_iota(jnp.int32, (1, LANES), 1) < width - last
    lane = lax.broadcasted_iota(jnp.int32, (1, LANES), 1)
    count = jnp.sum(jnp.where(lane == width - last, gram[pl.ds(width, 8), pl.ds(last, LANES)][0:1], 0.0))

    def clear(i, _):
        at = pl.ds(pl.multiple_of(i * TILE, TILE), TILE)
        gram[at, pl.ds(last, LANES)] = jnp.where(inside, gram[at, pl.ds(last, LANES)], 0.0)
        return 0

    lax.fori_loop(0, tiles, clear, 0)
    gram[pl.ds(width, wide - width), :] = jnp.zeros((wide - width, wide), F32)
    diagonal = jnp.zeros((LANES, LANES), F32)
    for b in range(wide // LANES):
        diagonal += gram[b * LANES : (b + 1) * LANES, b * LANES : (b + 1) * LANES] * eye
    trace = jnp.sum(diagonal)
    lift = damping[0] * trace / width
    unit = width / trace
    for b in range(wide // LANES):
        at = slice(b * LANES, (b + 1) * LANES)
        gram[at, at] += lift * (eye if b < wide // LANES - 1 else jnp.where(inside, eye, 0.0))

    blocks = wide // LANES

    def multiply(_, carry):
        factors = [vectors[1, :, b * LANES : (b + 1) * LANES] for b in range(blocks)]
        vectors[0] = vectors[1]
        for i in range(blocks):
            parts = []
            for q in range(LANES // 8):
                at = slice(i * LANES + q * 8, i * LANES + q * 8 + 8)
                total = gram[at, :LANES] * factors[0]
                for b in range(1, blocks):
                    total += gram[at, b * LANES : (b + 1) * LANES] * factors[b]
                parts.append(total)
            total = jnp.sum(jnp.concatenate(parts, axis=0).T, axis=0, keepdims=True) * unit
            vectors[1, :, i * LANES : (i + 1) * LANES] = jnp.broadcast_to(total, (8, LANES))
        return carry

    def half_turns(_, carry):
        lax.fori_loop(0, POWER // 2, multiply, 0)
        size = lax.rsqrt(jnp.sum(vectors[1] * vectors[1]) * 0.125)
        vectors[...] = vectors[...] * size
        return carry

    lane_all = lax.broadcasted_iota(jnp.int32, (8, wide), 1)
    vectors[1] = jnp.where(lane_all < width, 1.0 / math.sqrt(width), 0.0).astype(F32)
    lax.fori_loop(0, 2, half_turns, 0)
    before, vector = vectors[0], vectors[1]
    bound = 1.1 * (jnp.sum(before * vector) / jnp.sum(before * before))
    scale[0, 0] = bound * (trace / (count * width))
    rate = unit / bound

    def normalize(i, _):
        at = pl.ds(pl.multiple_of(i * LANES, LANES), LANES)
        t_all[at, :] = (gram[at, :] * (-0.5 * rate)).astype(BF16)
        return 0

    lax.fori_loop(0, blocks, normalize, 0)
    parts = []
    for b in range(blocks):
        at = slice(b * LANES, (b + 1) * LANES)
        ones = eye if b < blocks - 1 else jnp.where(inside, eye, 0.0)
        y_part = (gram[at, at] * rate).astype(BF16).astype(F32)
        t_part = ((3.0 * ones - y_part) * 0.5).astype(BF16)
        t_all[at, at] = t_part
        parts.append(jnp.sum((y_part + 2.0 * t_part.astype(F32)) * eye, axis=0, keepdims=True))
    lift_back = jnp.concatenate(parts, axis=1)

    first = member * rows
    t_rows[...] = t_all[pl.ds(pl.multiple_of(first, 16), rows), :]
    square = jnp.dot(t_rows[...], t_all[...], preferred_element_type=F32)
    a_rows[...] = (t_rows[...].astype(F32) * lift_back - 2.0 * square).astype(BF16)
    m_rows = jnp.dot(a_rows[...], t_all[...], preferred_element_type=F32)
    row = lax.broadcasted_iota(jnp.int32, (rows, wide), 0) + first
    col = lax.broadcasted_iota(jnp.int32, (rows, wide), 1)
    t_next[...] = (jnp.where(row == col, 1.5, 0.0) - 0.5 * m_rows).astype(BF16)
    out[...] = jnp.dot(t_next[...], t_all[...], preferred_element_type=F32)[:, :width]

    for step in range(16):
        plane_each(step, lambda copy: copy.wait_send())
        z_finish(step)

        @pl.when(direct(step))
        def _():
            pass_copy(step).wait_send()


def per_device(samples, routes, damping):
    members = lax.axis_size("grp")
    _, slots, strip, width = samples.shape
    wide = -(-width // TILE) * TILE
    rows = width // members
    vmem = pl.BlockSpec(memory_space=pltpu.VMEM)
    smem = pl.BlockSpec(memory_space=pltpu.SMEM)
    dma = pltpu.SemaphoreType.DMA
    result, scale = pl.pallas_call(
        functools.partial(fused, width, strip, slots),
        out_shape=(jax.ShapeDtypeStruct((rows, width), F32), jax.ShapeDtypeStruct((1, 1), F32)),
        in_specs=[vmem, vmem, smem],
        out_specs=(vmem, smem),
        scratch_shapes=[
            pltpu.VMEM((slots * strip, wide), BF16),
            pltpu.VMEM((32, 2 * strip, wide), BF16),
            pltpu.VMEM((32, 2 * strip, wide), BF16),
            pltpu.VMEM((32, 2 * strip, wide), BF16),
            pltpu.VMEM((128, 2 * strip, wide), BF16),
            pltpu.VMEM((wide, wide), F32),
            pltpu.VMEM((wide, wide), BF16),
            pltpu.VMEM((rows, wide), BF16),
            pltpu.VMEM((rows, wide), BF16),
            pltpu.VMEM((rows, wide), BF16),
            pltpu.VMEM((2, 8, wide), F32),
            dma((16, 2)),
            dma((16, 2)),
            dma((16, 4)),
            dma((16,)),
            dma((16,)),
            dma((16,)),
        ],
        compiler_params=pltpu.CompilerParams(
            collective_id=0, has_side_effects=True, vmem_limit_bytes=60 * 1024 * 1024
        ),
        name="inverse_root",
    )(samples.reshape(slots * strip, width), routes.reshape(1, slots), damping)
    return (result[None], scale.reshape(1))


def solution(mesh):
    in_specs = (P("grp", "wide", None, None), P("grp", "wide", None), P("wide"))
    out_specs = (P("wide", "grp", None), P("wide"))
    return jax.shard_map(
        per_device, mesh=mesh, in_specs=in_specs, out_specs=out_specs, check_vma=False
    )
```

time: 144 us -> 124 us (0.86)
  Pallas kernels: 132 us -> 117 us
  other arithmetic: 2.65 us -> 0 us
  local copies, waits for them, and re-layouts: 5.21 us -> 3.72 us
    pallas_call x1, Pallas kernels: 132 us -> 117 us  [per_device(): pl.pallas_call(functools.partial(fused, width, strip, slots), out_shape=(...]
    concatenate x1 -> x0, other arithmetic: 2.65 us -> none  [per_device(): ext = jnp.concatenate([strips, mark], axis=1)]
where the time goes in v2:
time: 124 us
  Pallas kernels  117 us (94%)
  local copies, waits for them, and re-layouts  3.72 us (3%)
  between operations  3.1 us (2%)
    pallas_call x1, Pallas kernels, per_device(): pl.pallas_call(functools.partial(fused, width, strip, slots), out_shape=(...  117 us
    unnamed x1, local copies, waits for them, and re-layouts  3.72 us

profile of v2, /device:TPU:1, one launch (start us, length us, event | category | flops | bytes accessed | tf_op | source)
XLA Modules:
  0.0 124.0 jit_solution(17883484461941808518)
XLA Ops:
  1.3 117.2 %inverse_root.1 = (f32[432,1728]{1,0:T(8,128)}, f32[1,1]{1,0:T(1,128)}) custom-call(bf16[384,1728]{1,0:T(8,128)(2,1)} %bitcast.5, s32[1,48]{1,0:T(1,128)} %bitcast.6, f32[1]{0:T(128)S(6)} %copy.7.damping), custom_call_target="tpu_custom_call" | custom-call | tf_op jit(solution)/shard_map/inverse_root/pallas_call | solution.py:307
  118.4 3.7 %copy.8 = f32[1,432,1728]{2,1,0:T(8,128)} copy(f32[1,432,1728]{2,1,0:T(8,128)} %bitcast.4) | data formatting | bytes 5971968

commit v3 on v2

--- a/solution.py
+++ b/solution.py
@@ -25,7 +25,7 @@
     return (lax.div(z, 4) * 2 + core, x * 16 + lax.rem(z, 4) * 4 + y)
 
 
-def fused(width, strip, slots, strips, routes, damping, out, scale, ext, chosen, staged, cells, stack, gram, t_all, t_rows, a_rows, t_next, vectors, plane_send, plane_recv, z_send, group_recv, pass_send, pass_recv):
+def collect(width, strip, slots, strips, routes, damping, gram, stats, ext, chosen, staged, cells, stack, plane_send, plane_recv, z_send, group_recv, pass_send, pass_recv):
     member, worker = lax.axis_index("grp"), lax.axis_index("wide")
     core = lax.rem(member, 2)
     x, y = lax.div(worker, 16), lax.rem(worker, 4)
@@ -33,7 +33,6 @@
     even = lax.rem(z, 2) == core
     wide = ext.shape[1]
     tiles = wide // TILE
-    rows = out.shape[0]
     pair_rows = 2 * strip
     last = wide - LANES
 
@@ -225,12 +224,33 @@
         diagonal += gram[b * LANES : (b + 1) * LANES, b * LANES : (b + 1) * LANES] * eye
     trace = jnp.sum(diagonal)
     lift = damping[0] * trace / width
-    unit = width / trace
+    stats[0, 0] = trace
+    stats[0, 1] = count
     for b in range(wide // LANES):
         at = slice(b * LANES, (b + 1) * LANES)
         gram[at, at] += lift * (eye if b < wide // LANES - 1 else jnp.where(inside, eye, 0.0))
 
+    for step in range(16):
+        plane_each(step, lambda copy: copy.wait_send())
+        z_finish(step)
+
+        @pl.when(direct(step))
+        def _():
+            pass_copy(step).wait_send()
+
+
+def invert(width, gram, stats, out, scale, t_all, t_rows, a_rows, t_next, vectors):
+    member = lax.axis_index("grp")
+    wide, rows = gram.shape[1], out.shape[0]
+    last = wide - LANES
+
     blocks = wide // LANES
+    trace = stats[0, 0]
+    unit = width / trace
+    eye = (
+        lax.broadcasted_iota(jnp.int32, (LANES, LANES), 0) == lax.broadcasted_iota(jnp.int32, (LANES, LANES), 1)
+    ).astype(F32)
+    inside = lax.broadcasted_iota(jnp.int32, (1, LANES), 1) < width - last
 
     def multiply(_, carry):
         factors = [vectors[1, :, b * LANES : (b + 1) * LANES] for b in range(blocks)]
@@ -258,7 +278,7 @@
     lax.fori_loop(0, 2, half_turns, 0)
     before, vector = vectors[0], vectors[1]
     bound = 1.1 * (jnp.sum(before * vector) / jnp.sum(before * before))
-    scale[0, 0] = bound * (trace / (count * width))
+    scale[0, 0] = bound * (trace / (stats[0, 1] * width))
     rate = unit / bound
 
     def normalize(i, _):
@@ -287,13 +307,26 @@
     t_next[...] = (jnp.where(row == col, 1.5, 0.0) - 0.5 * m_rows).astype(BF16)
     out[...] = jnp.dot(t_next[...], t_all[...], preferred_element_type=F32)[:, :width]
 
-    for step in range(16):
-        plane_each(step, lambda copy: copy.wait_send())
-        z_finish(step)
-
-        @pl.when(direct(step))
-        def _():
-            pass_copy(step).wait_send()
+
+def invert_call(gram, stats, width, rows):
+    wide = gram.shape[1]
+    vmem = pl.BlockSpec(memory_space=pltpu.VMEM)
+    smem = pl.BlockSpec(memory_space=pltpu.SMEM)
+    return pl.pallas_call(
+        functools.partial(invert, width),
+        out_shape=(jax.ShapeDtypeStruct((rows, width), F32), jax.ShapeDtypeStruct((1, 1), F32)),
+        in_specs=[vmem, smem],
+        out_specs=(vmem, smem),
+        scratch_shapes=[
+            pltpu.VMEM((wide, wide), BF16),
+            pltpu.VMEM((rows, wide), BF16),
+            pltpu.VMEM((rows, wide), BF16),
+            pltpu.VMEM((rows, wide), BF16),
+            pltpu.VMEM((2, 8, wide), F32),
+        ],
+        compiler_params=pltpu.CompilerParams(vmem_limit_bytes=36 * 1024 * 1024),
+        name="invert",
+    )(gram, stats)
 
 
 def per_device(samples, routes, damping):
@@ -304,9 +337,9 @@
     vmem = pl.BlockSpec(memory_space=pltpu.VMEM)
     smem = pl.BlockSpec(memory_space=pltpu.SMEM)
     dma = pltpu.SemaphoreType.DMA
-    result, scale = pl.pallas_call(
-        functools.partial(fused, width, strip, slots),
-        out_shape=(jax.ShapeDtypeStruct((rows, width), F32), jax.ShapeDtypeStruct((1, 1), F32)),
+    gram, stats = pl.pallas_call(
+        functools.partial(collect, width, strip, slots),
+        out_shape=(pltpu.VMEM((wide, wide), F32), jax.ShapeDtypeStruct((1, 2), F32)),
         in_specs=[vmem, vmem, smem],
         out_specs=(vmem, smem),
         scratch_shapes=[
@@ -315,12 +348,6 @@
             pltpu.VMEM((32, 2 * strip, wide), BF16),
             pltpu.VMEM((32, 2 * strip, wide), BF16),
             pltpu.VMEM((128, 2 * strip, wide), BF16),
-            pltpu.VMEM((wide, wide), F32),
-            pltpu.VMEM((wide, wide), BF16),
-            pltpu.VMEM((rows, wide), BF16),
-            pltpu.VMEM((rows, wide), BF16),
-            pltpu.VMEM((rows, wide), BF16),
-            pltpu.VMEM((2, 8, wide), F32),
             dma((16, 2)),
             dma((16, 2)),
             dma((16, 4)),
@@ -329,10 +356,11 @@
             dma((16,)),
         ],
         compiler_params=pltpu.CompilerParams(
-            collective_id=0, has_side_effects=True, vmem_limit_bytes=60 * 1024 * 1024
+            collective_id=0, has_side_effects=True, vmem_limit_bytes=26 * 1024 * 1024
         ),
-        name="inverse_root",
+        name="collect",
     )(samples.reshape(slots * strip, width), routes.reshape(1, slots), damping)
+    result, scale = invert_call(gram, stats, width, rows)
     return (result[None], scale.reshape(1))
 
 

time: 124 us -> 121 us (0.976)
  local copies, waits for them, and re-layouts: 3.72 us -> 1.99 us
  between operations: 3.1 us -> 1.47 us
    unnamed x1 -> x4, local copies, waits for them, and re-layouts: 3.72 us -> 1.99 us
    pallas_call x1 -> x2, Pallas kernels: 117 us -> 117 us  [the longest x1 98.6 us: per_device(): pl.pallas_call(functools.partial(collect, width, strip, slots), out_shape...]
where the time goes in v3:
time: 121 us
  Pallas kernels  117 us (97%)
  local copies, waits for them, and re-layouts  1.99 us (2%)
  between operations  1.47 us (1%)
    pallas_call x1, Pallas kernels, per_device(): pl.pallas_call(functools.partial(collect, width, strip, slots), out_shape...  98.6 us
    pallas_call x1, Pallas kernels, invert_call(): pl.pallas_call(functools.partial(invert, width), out_shape=(jax.ShapeDtyp...  18.7 us

profile of v3, /device:TPU:1, one launch (start us, length us, event | category | flops | bytes accessed | tf_op | source)
XLA Modules:
  0.0 120.8 jit_solution(8141983276428385661)
XLA Ops:
  1.3 0.0 copy-start
  1.3 1.3 %copy-done = bf16[1,48,8,1728]{3,2,1,0:T(8,128)(2,1)S(1)} copy-done((bf16[1,48,8,1728]{3,2,1,0:T(8,128)(2,1)S(1)}, bf16[1,48,8,1728]{3,2,1,0:T(8,128)(2,1)}, u32[]{:S(2)}) %copy-start) | copy-done | bytes 1327128
  2.6 0.0 copy-start.1
  2.6 0.7 copy-done.1
  3.3 98.6 %collect.1 = (f32[1792,1792]{1,0:T(8,128)S(1)}, f32[1,2]{1,0:T(1,128)S(1)}) custom-call(bf16[384,1728]{1,0:T(8,128)(2,1)S(1)} %bitcast.4, s32[1,48]{1,0:T(1,128)S(1)} %bitcast.5, f32[1]{0:T(128)S(6)} %copy.5.damping), custom_call_target="tpu_custom_call" | custom-call | tf_op jit(solution)/shard_map/collect/pallas_call | solution.py:340
  101.9 18.7 %invert.1 = (f32[432,1728]{1,0:T(8,128)}, f32[1,1]{1,0:T(1,128)}) custom-call(f32[1792,1792]{1,0:T(8,128)S(1)} %get-tuple-element.6.gram, f32[1,2]{1,0:T(1,128)S(1)} %get-tuple-element.7.stats), custom_call_target="tpu_custom_call" | custom-call | tf_op jit(solution)/shard_map/invert/pallas_call | solution.py:315
Async XLA Ops:
  1.3 1.3 %copy-start = (bf16[1,48,8,1728]{3,2,1,0:T(8,128)(2,1)S(1)}, bf16[1,48,8,1728]{3,2,1,0:T(8,128)(2,1)}, u32[]{:S(2)}) copy-start(bf16[1,48,8,1728]{3,2,1,0:T(8,128)(2,1)} %param.3) | copy-start | bytes 3981316
  2.6 0.7 copy-start.1

commit v4 on v3

v4 whole, which is shorter than its diff:
```python
import functools
import math

import jax
import jax.numpy as jnp
from jax import lax
from jax.experimental import pallas as pl
from jax.experimental.pallas import tpu as pltpu
from jax.sharding import PartitionSpec as P

POWER = 6
MESH = pl.DeviceIdType.MESH
F32, BF16 = jnp.float32, jnp.bfloat16
LANES = 128
TILE = 256

STEPS = (
    (0, 0), (1, 0), (1, 1), (3, 0), (3, 3), (0, 1), (1, 3), (0, 3),
    (3, 1), (2, 1), (2, 0), (1, 2), (0, 2), (2, 3), (2, 2), (3, 2),
)
LAG = 6


def device(z, core, x, y):
    return (lax.div(z, 4) * 2 + core, x * 16 + lax.rem(z, 4) * 4 + y)


def collect(width, strip, slots, strips_hbm, routes_hbm, damping, gram, stats, strips, routes, ext, chosen, staged, cells, ends, held, flags, stack, strays, load_sem, plane_send, plane_recv, z_send, group_recv, pass_send, pass_recv, end_send, end_recv, over_send, over_recv):
    member, worker = lax.axis_index("grp"), lax.axis_index("wide")
    core = lax.rem(member, 2)
    x, y = lax.div(worker, 16), lax.rem(worker, 4)
    z = lax.div(member, 2) * 4 + lax.rem(lax.div(worker, 4), 4)
    even = lax.rem(z, 2) == core
    wide = ext.shape[1]
    pair_rows = 2 * strip
    last = wide - LANES

    def peer(dx, dy):
        return lax.rem(x + dx, 4), lax.rem(y + dy, 4)

    loads = [
        pltpu.make_async_copy(strips_hbm, strips, load_sem.at[0]),
        pltpu.make_async_copy(routes_hbm, routes, load_sem.at[1]),
    ]
    for load in loads:
        load.start()

    barrier = pltpu.get_barrier_semaphore()
    pl.semaphore_signal(barrier, inc=1, device_id=device(z, 1 - core, x, y), device_id_type=MESH)
    for dx, dy in STEPS[1:]:
        px, py = peer(dx, dy)
        for there in range(2):
            pl.semaphore_signal(barrier, inc=1, device_id=device(z, there, px, py), device_id_type=MESH)
    for dz in range(1, 8):
        pl.semaphore_signal(barrier, inc=1, device_id=device(lax.rem(z + dz, 8), lax.rem(z, 2), x, y), device_id_type=MESH)

    for load in loads:
        load.wait()
    ext[:, :last] = strips[:, :last]
    mark = lax.broadcasted_iota(jnp.int32, (slots * strip, wide - width), 1) == 0
    ext[:, last:] = jnp.concatenate([strips[:, last:].astype(F32), jnp.where(mark, 1.0, 0.0)], axis=1).astype(BF16)
    spread = lax.broadcasted_iota(jnp.int32, (slots, slots * strip), 1) // strip == lax.broadcasted_iota(
        jnp.int32, (slots, slots * strip), 0
    )
    named = jnp.broadcast_to(routes[...].astype(F32), (8, slots)).astype(BF16)
    named = jnp.dot(named, jnp.where(spread, 1.0, 0.0).astype(BF16), preferred_element_type=F32)[0:1].astype(jnp.int32)
    shape = (32 * pair_rows, slots * strip)
    row = lax.broadcasted_iota(jnp.int32, shape, 0)
    col = lax.broadcasted_iota(jnp.int32, shape, 1)
    place, plane = row // (2 * pair_rows), 2 * ((row // strip) % 2) + (row // pair_rows) % 2
    factor = (place // 4) * 16 + plane * 4 + place % 4
    pick = jnp.where((named == factor) & (row % strip == col % strip), 1.0, 0.0).astype(BF16)
    chosen[...] = jnp.dot(pick, ext[...], preferred_element_type=F32).astype(BF16).reshape(32, pair_rows, wide)
    pl.semaphore_wait(barrier, jnp.where(even, 37, 39))

    def plane_copy(step, there):
        px, py = peer(*STEPS[step])
        return pltpu.make_async_remote_copy(
            chosen.at[2 * (px * 4 + py) + there],
            staged.at[2 * step + core],
            plane_send.at[step, there],
            plane_recv.at[step, core],
            device_id=device(z, there, px, py),
            device_id_type=MESH,
        )

    def plane_each(step, act):
        for there in range(2):
            if step > 0:
                act(plane_copy(step, there))
            else:

                @pl.when(core != there)
                def _():
                    act(plane_copy(step, there))

    def plane_wait(step):
        for source in range(2):
            landed = staged.at[2 * step + source]
            if step > 0:
                pltpu.make_async_copy(landed, landed, plane_recv.at[step, source]).wait()
            else:

                @pl.when(core != source)
                def _():
                    pltpu.make_async_copy(landed, landed, plane_recv.at[step, source]).wait()

    for step in range(16):
        plane_each(step, lambda copy: copy.start())
    staged[core] = chosen[2 * (x * 4 + y) + core]

    def origin(step):
        dx, dy = STEPS[step]
        return peer(4 - dx, 4 - dy)

    def direct(step):
        sx, sy = origin(step)
        return lax.rem(sx + sy, 2) == core

    def end_step(entry):
        return 4 * (entry // 2) + 2 + entry % 2 if entry < 8 else 15

    def z_copy(step, dz, slot, near=False, entry=None):
        sx, sy = origin(step)
        target = lax.rem(z + dz, 8)
        j = lax.div(lax.rem(target, 4), 2)
        if entry is None:
            source, landing = cells.at[2 * step + j], stack.at[step * 8 + z]
            sent, landed = z_send.at[step, slot], group_recv.at[step]
        else:
            source, landing = ends.at[2 * entry + j], strays.at[entry * 8 + z]
            sent, landed = end_send.at[entry, slot], end_recv.at[entry]
        if near:
            return pltpu.make_async_copy(source, landing, landed)
        return pltpu.make_async_remote_copy(
            source,
            landing,
            sent,
            landed,
            device_id=device(target, lax.rem(sx + sy, 2), x, y),
            device_id_type=MESH,
        )

    def z_spread(step, entry=None):
        @pl.when(even)
        def _():
            for slot, dz in enumerate((4, 2, 6)):
                z_copy(step, dz, slot, entry=entry).start()

            @pl.when(direct(step))
            def _():
                z_copy(step, 0, 3, near=True, entry=entry).start()

            @pl.when(jnp.logical_not(direct(step)))
            def _():
                z_copy(step, 0, 3, entry=entry).start()

        @pl.when(jnp.logical_not(even))
        def _():
            for slot, dz in enumerate((5, 3, 1, 7)):
                z_copy(step, dz, slot, entry=entry).start()

    def z_start(step):
        plane_wait(step)
        one, two = staged[2 * step].astype(F32), staged[2 * step + 1].astype(F32)
        for j in range(2):
            part = slice(j * strip, (j + 1) * strip)
            cell = jnp.concatenate([one[part], two[part]], 0)
            cells[2 * step + j] = cell[:, :last].astype(BF16)
            end = cell[:, last:]
            flags[j] = end if step == 0 else flags[j] + end
            if step % 4 < 2:
                held[2 * (step % 2) + j] = end
            else:
                entry = 2 * (step // 4) + step % 2
                former = held[2 * (step % 2) + j]
                ends[2 * entry + j] = jnp.concatenate([former[:, : width - last], end[:, : width - last]], 1).astype(BF16)
        z_spread(step)
        if step % 4 >= 2:
            z_spread(step, 2 * (step // 4) + step % 2)
        if step == 15:
            lane = lax.broadcasted_iota(jnp.int32, (pair_rows, LANES), 1)
            for j in range(2):
                total = jnp.sum(jnp.where(lane == width - last, flags[j], 0.0))
                ends[16 + j] = jnp.broadcast_to(total, (pair_rows, LANES)).astype(BF16)
            z_spread(step, 8)

    def z_finish(step, entry=None):
        for slot in range(3):
            z_copy(step, 1, slot, entry=entry).wait_send()

        @pl.when(jnp.logical_not(even & direct(step)))
        def _():
            z_copy(step, 1, 3, entry=entry).wait_send()

    sibling = device(z, 1 - core, x, y)

    def pass_copy(step, entry=None):
        if entry is None:
            group, sent, landed = stack.at[pl.ds(step * 8, 8)], pass_send.at[step], pass_recv.at[step]
        else:
            group, sent, landed = strays.at[pl.ds(entry * 8, 8)], over_send.at[entry], over_recv.at[entry]
        return pltpu.make_async_remote_copy(
            group, group, sent, landed, device_id=sibling, device_id_type=MESH
        )

    def arrive(step, entry=None):
        if entry is None:
            group, landed = stack.at[pl.ds(step * 8, 8)], group_recv.at[step]
        else:
            group, landed = strays.at[pl.ds(entry * 8, 8)], end_recv.at[entry]

        @pl.when(direct(step))
        def _():
            pltpu.make_async_copy(group, group, landed).wait()
            pass_copy(step, entry).start()

    def passed(step, entry=None):
        @pl.when(jnp.logical_not(direct(step)))
        def _():
            pass_copy(step, entry).wait_recv()

    def pass_finish(step, entry=None):
        @pl.when(direct(step))
        def _():
            pass_copy(step, entry).wait_send()

    depth, middle = 16 * pair_rows, wide // 2

    def accumulate(pair):
        for start, stop in ((0, middle), (middle, last)):
            left = stack[pl.ds(pair * 16, 16), :, start:stop].reshape(depth, stop - start)
            block = stack[pl.ds(pair * 16, 16)].reshape(depth, last)
            term = lax.dot_general(left, block, (((0,), (0,)), ((), ())), preferred_element_type=F32)
            if pair == 0:
                gram[start:stop, :last] = term
            else:
                gram[start:stop, :last] += term

    def accumulate_ends(quad):
        blank = jnp.zeros((8 * pair_rows, wide - width), F32)
        parts = []
        for i in range(4):
            pair_of = strays[pl.ds((2 * quad + i % 2) * 8, 8)].reshape(8 * pair_rows, LANES).astype(F32)
            kept = pair_of[:, : width - last] if i < 2 else pair_of[:, width - last :]
            parts.append(jnp.concatenate([kept, blank], 1))
        left = jnp.concatenate(parts, 0).astype(BF16)
        block = stack[pl.ds(quad * 32, 32)].reshape(2 * depth, last)
        for where, right in ((slice(0, last), block), (slice(last, wide), left)):
            term = lax.dot_general(left, right, (((0,), (0,)), ((), ())), preferred_element_type=F32)
            if quad == 0:
                gram[last:, where] = term
            else:
                gram[last:, where] += term

    def entries(pair):
        return [entry for entry in range(9) if end_step(entry) // 2 == pair]

    for turn in range(8 + LAG // 2):
        if turn < 8:
            z_start(2 * turn)
            z_start(2 * turn + 1)
        if turn >= LAG // 2:
            pair = turn - LAG // 2
            items = [(step, None) for step in (2 * pair, 2 * pair + 1)]
            items += [(end_step(entry), entry) for entry in entries(pair)]
            for item in items:
                arrive(*item)
            if turn == 8:
                for step in range(16):
                    plane_each(step, lambda copy: copy.wait_send())
            done = {8: range(4), 9: range(4, 6), 10: range(6, 8)}.get(turn, ())
            for other in done:
                for item in [(step, None) for step in (2 * other, 2 * other + 1)]:
                    z_finish(*item)
                for entry in entries(other):
                    z_finish(end_step(entry), entry)
                if other < 7:
                    for item in [(step, None) for step in (2 * other, 2 * other + 1)]:
                        pass_finish(*item)
                    for entry in entries(other):
                        pass_finish(end_step(entry), entry)
            for item in items:
                passed(*item)
            accumulate(pair)
            if pair % 2:
                accumulate_ends(pair // 2)
    for item in items:
        pass_finish(*item)

    for b in range(last // LANES):
        gram[b * LANES : (b + 1) * LANES, last:] = gram[last:, b * LANES : (b + 1) * LANES].T
    eye = (
        lax.broadcasted_iota(jnp.int32, (LANES, LANES), 0) == lax.broadcasted_iota(jnp.int32, (LANES, LANES), 1)
    ).astype(F32)
    inside = lax.broadcasted_iota(jnp.int32, (1, LANES), 1) < width - last
    count = jnp.sum(strays[64:].astype(F32)) * (1.0 / (pair_rows * LANES))
    diagonal = jnp.zeros((LANES, LANES), F32)
    for b in range(wide // LANES):
        diagonal += gram[b * LANES : (b + 1) * LANES, b * LANES : (b + 1) * LANES] * eye
    trace = jnp.sum(diagonal)
    lift = damping[0] * trace / width
    stats[0, 0] = trace
    stats[0, 1] = count
    for b in range(wide // LANES):
        at = slice(b * LANES, (b + 1) * LANES)
        gram[at, at] += lift * (eye if b < wide // LANES - 1 else jnp.where(inside, eye, 0.0))


def invert(width, gram, stats, out, scale, t_all, t_rows, a_rows, t_next, vectors):
    wide, rows = gram.shape[1], out.shape[0]
    half = out.shape[1]
    last = wide - LANES
    first = lax.axis_index("grp") * rows

    @pl.when(pl.program_id(0) == 0)
    def _():
        blocks = wide // LANES
        trace = stats[0, 0]
        unit = width / trace
        eye = (
            lax.broadcasted_iota(jnp.int32, (LANES, LANES), 0) == lax.broadcasted_iota(jnp.int32, (LANES, LANES), 1)
        ).astype(F32)
        inside = lax.broadcasted_iota(jnp.int32, (1, LANES), 1) < width - last

        def multiply(_, carry):
            factors = [vectors[1, :, b * LANES : (b + 1) * LANES] for b in range(blocks)]
            vectors[0] = vectors[1]
            for i in range(blocks):
                parts = []
                for q in range(LANES // 8):
                    at = slice(i * LANES + q * 8, i * LANES + q * 8 + 8)
                    total = gram[at, :LANES] * factors[0]
                    for b in range(1, blocks):
                        total += gram[at, b * LANES : (b + 1) * LANES] * factors[b]
                    parts.append(total)
                total = jnp.sum(jnp.concatenate(parts, axis=0).T, axis=0, keepdims=True) * unit
                vectors[1, :, i * LANES : (i + 1) * LANES] = jnp.broadcast_to(total, (8, LANES))
            return carry

        def half_turns(_, carry):
            lax.fori_loop(0, POWER // 2, multiply, 0)
            size = lax.rsqrt(jnp.sum(vectors[1] * vectors[1]) * 0.125)
            vectors[...] = vectors[...] * size
            return carry

        lane_all = lax.broadcasted_iota(jnp.int32, (8, wide), 1)
        vectors[1] = jnp.where(lane_all < width, 1.0 / math.sqrt(width), 0.0).astype(F32)
        lax.fori_loop(0, 2, half_turns, 0)
        before, vector = vectors[0], vectors[1]
        bound = 1.1 * (jnp.sum(before * vector) / jnp.sum(before * before))
        scale[0, 0] = bound * (trace / (stats[0, 1] * width))
        rate = unit / bound

        def normalize(i, _):
            at = pl.ds(pl.multiple_of(i * LANES, LANES), LANES)
            t_all[at, :] = (gram[at, :] * (-0.5 * rate)).astype(BF16)
            return 0

        lax.fori_loop(0, blocks, normalize, 0)
        parts = []
        for b in range(blocks):
            at = slice(b * LANES, (b + 1) * LANES)
            ones = eye if b < blocks - 1 else jnp.where(inside, eye, 0.0)
            y_part = (gram[at, at] * rate).astype(BF16).astype(F32)
            t_part = ((3.0 * ones - y_part) * 0.5).astype(BF16)
            t_all[at, at] = t_part
            parts.append(jnp.sum((y_part + 2.0 * t_part.astype(F32)) * eye, axis=0, keepdims=True))
        lift_back = jnp.concatenate(parts, axis=1)

        t_rows[...] = t_all[pl.ds(pl.multiple_of(first, 16), rows), :]
        square = jnp.dot(t_rows[...], t_all[...], preferred_element_type=F32)
        a_rows[...] = (t_rows[...].astype(F32) * lift_back - 2.0 * square).astype(BF16)
        m_rows = jnp.dot(a_rows[...], t_all[...], preferred_element_type=F32)
        row = lax.broadcasted_iota(jnp.int32, (rows, wide), 0) + first
        col = lax.broadcasted_iota(jnp.int32, (rows, wide), 1)
        t_next[...] = (jnp.where(row == col, 1.5, 0.0) - 0.5 * m_rows).astype(BF16)
        out[...] = jnp.dot(t_next[...], t_all[:, :half], preferred_element_type=F32)

    @pl.when(pl.program_id(0) == 1)
    def _():
        out[...] = jnp.dot(t_next[...], t_all[:, half:], preferred_element_type=F32)


def invert_call(gram, stats, width, rows):
    wide = gram.shape[1]
    vmem = pl.BlockSpec(memory_space=pltpu.VMEM)
    smem = pl.BlockSpec(memory_space=pltpu.SMEM)
    return pl.pallas_call(
        functools.partial(invert, width),
        out_shape=(jax.ShapeDtypeStruct((rows, width), F32), jax.ShapeDtypeStruct((1, 1), F32)),
        grid=(2,),
        in_specs=[vmem, smem],
        out_specs=(pl.BlockSpec((rows, wide // 2), lambda i: (0, i)), smem),
        scratch_shapes=[
            pltpu.VMEM((wide, wide), BF16),
            pltpu.VMEM((rows, wide), BF16),
            pltpu.VMEM((rows, wide), BF16),
            pltpu.VMEM((rows, wide), BF16),
            pltpu.VMEM((2, 8, wide), F32),
        ],
        compiler_params=pltpu.CompilerParams(vmem_limit_bytes=36 * 1024 * 1024),
        name="invert",
    )(gram, stats)


def per_device(samples, routes, damping):
    members = lax.axis_size("grp")
    _, slots, strip, width = samples.shape
    wide = -(-width // TILE) * TILE
    rows = width // members
    vmem = pl.BlockSpec(memory_space=pltpu.VMEM)
    smem = pl.BlockSpec(memory_space=pltpu.SMEM)
    hbm = pl.BlockSpec(memory_space=pltpu.HBM)
    dma = pltpu.SemaphoreType.DMA
    gram, stats = pl.pallas_call(
        functools.partial(collect, width, strip, slots),
        out_shape=(pltpu.VMEM((wide, wide), F32), jax.ShapeDtypeStruct((1, 2), F32)),
        in_specs=[hbm, hbm, smem],
        out_specs=(vmem, smem),
        scratch_shapes=[
            pltpu.VMEM((slots * strip, width), BF16),
            pltpu.VMEM((1, slots), jnp.int32),
            pltpu.VMEM((slots * strip, wide), BF16),
            pltpu.VMEM((32, 2 * strip, wide), BF16),
            pltpu.VMEM((32, 2 * strip, wide), BF16),
            pltpu.VMEM((32, 2 * strip, wide - LANES), BF16),
            pltpu.VMEM((18, 2 * strip, LANES), BF16),
            pltpu.VMEM((4, 2 * strip, LANES), F32),
            pltpu.VMEM((2, 2 * strip, LANES), F32),
            pltpu.VMEM((128, 2 * strip, wide - LANES), BF16),
            pltpu.VMEM((72, 2 * strip, LANES), BF16),
            dma((2,)),
            dma((16, 2)),
            dma((16, 2)),
            dma((16, 4)),
            dma((16,)),
            dma((16,)),
            dma((16,)),
            dma((9, 4)),
            dma((9,)),
            dma((9,)),
            dma((9,)),
        ],
        compiler_params=pltpu.CompilerParams(
            collective_id=0, has_side_effects=True, vmem_limit_bytes=26 * 1024 * 1024
        ),
        name="collect",
    )(
        pltpu.with_memory_space_constraint(samples.reshape(slots * strip, width), pltpu.HBM),
        pltpu.with_memory_space_constraint(routes.reshape(1, slots), pltpu.HBM),
        damping,
    )
    result, scale = invert_call(gram, stats, width, rows)
    return (result[None], scale.reshape(1))


def solution(mesh):
    in_specs = (P("grp", "wide", None, None), P("grp", "wide", None), P("wide"))
    out_specs = (P("wide", "grp", None), P("wide"))
    return jax.shard_map(
        per_device, mesh=mesh, in_specs=in_specs, out_specs=out_specs, check_vma=False
    )
```

time: 121 us -> 117 us (0.967)
  local copies, waits for them, and re-layouts: 1.99 us -> 0 us
    unnamed x4 -> x0, local copies, waits for them, and re-layouts: 1.99 us -> none
    pallas_call x1, Pallas kernels: 98.6 us -> 97.2 us  [per_device(): pl.pallas_call(functools.partial(collect, width, strip, slots), out_shape...]
where the time goes in v4:
time: 117 us
  Pallas kernels  116 us (99%)
  between operations  1.28 us (1%)
    pallas_call x1, Pallas kernels, per_device(): pl.pallas_call(functools.partial(collect, width, strip, slots), out_shape...  97.2 us
    pallas_call x1, Pallas kernels, invert_call(): pl.pallas_call(functools.partial(invert, width), out_shape=(jax.ShapeDtyp...  18.6 us

profile of v4, /device:TPU:1, one launch (start us, length us, event | category | flops | bytes accessed | tf_op | source)
XLA Modules:
  0.0 117.1 jit_solution(6462848562269725418)
XLA Ops:
  1.3 97.2 %collect.1 = (f32[1792,1792]{1,0:T(8,128)S(1)}, f32[1,2]{1,0:T(1,128)S(1)}) custom-call(bf16[384,1728]{1,0:T(8,128)(2,1)} %bitcast.4, s32[1,48]{1,0:T(1,128)} %bitcast.5, f32[1]{0:T(128)S(6)} %copy.5.damping), custom_call_target="tpu_custom_call" | custom-call | tf_op jit(solution)/shard_map/collect/pallas_call | solution.py:416
  98.5 18.6 %invert.1 = (f32[432,1728]{1,0:T(8,128)}, f32[1,1]{1,0:T(1,128)}) custom-call(f32[1792,1792]{1,0:T(8,128)S(1)} %get-tuple-element.6.gram, f32[1,2]{1,0:T(1,128)S(1)} %get-tuple-element.7.stats), custom_call_target="tpu_custom_call" | custom-call | tf_op jit(solution)/shard_map/invert/pallas_call | solution.py:389

commit v5 on v4

--- a/solution.py
+++ b/solution.py
@@ -309,7 +309,7 @@
 
 def invert(width, gram, stats, out, scale, t_all, t_rows, a_rows, t_next, vectors):
     wide, rows = gram.shape[1], out.shape[0]
-    half = out.shape[1]
+    share = out.shape[1]
     last = wide - LANES
     first = lax.axis_index("grp") * rows
 
@@ -352,12 +352,9 @@
         scale[0, 0] = bound * (trace / (stats[0, 1] * width))
         rate = unit / bound
 
-        def normalize(i, _):
-            at = pl.ds(pl.multiple_of(i * LANES, LANES), LANES)
+        for i in range(blocks):
+            at = slice(i * LANES, (i + 1) * LANES)
             t_all[at, :] = (gram[at, :] * (-0.5 * rate)).astype(BF16)
-            return 0
-
-        lax.fori_loop(0, blocks, normalize, 0)
         parts = []
         for b in range(blocks):
             at = slice(b * LANES, (b + 1) * LANES)
@@ -375,15 +372,16 @@
         row = lax.broadcasted_iota(jnp.int32, (rows, wide), 0) + first
         col = lax.broadcasted_iota(jnp.int32, (rows, wide), 1)
         t_next[...] = (jnp.where(row == col, 1.5, 0.0) - 0.5 * m_rows).astype(BF16)
-        out[...] = jnp.dot(t_next[...], t_all[:, :half], preferred_element_type=F32)
+        out[...] = jnp.dot(t_next[...], t_all[:, :share], preferred_element_type=F32)
 
     @pl.when(pl.program_id(0) == 1)
     def _():
-        out[...] = jnp.dot(t_next[...], t_all[:, half:], preferred_element_type=F32)
+        out[:, : wide - share] = jnp.dot(t_next[...], t_all[:, share:], preferred_element_type=F32)
 
 
 def invert_call(gram, stats, width, rows):
     wide = gram.shape[1]
+    share = -(-wide // (2 * TILE)) * TILE
     vmem = pl.BlockSpec(memory_space=pltpu.VMEM)
     smem = pl.BlockSpec(memory_space=pltpu.SMEM)
     return pl.pallas_call(
@@ -391,7 +389,7 @@
         out_shape=(jax.ShapeDtypeStruct((rows, width), F32), jax.ShapeDtypeStruct((1, 1), F32)),
         grid=(2,),
         in_specs=[vmem, smem],
-        out_specs=(pl.BlockSpec((rows, wide // 2), lambda i: (0, i)), smem),
+        out_specs=(pl.BlockSpec((rows, share), lambda i: (0, i)), smem),
         scratch_shapes=[
             pltpu.VMEM((wide, wide), BF16),
             pltpu.VMEM((rows, wide), BF16),

time: 117 us -> 117 us (level)
  no operation moved by 1% of the time
where the time goes in v5:
time: 117 us
  Pallas kernels  115 us (98%)
  between operations  1.28 us (1%)
    pallas_call x1, Pallas kernels, per_device(): pl.pallas_call(functools.partial(collect, width, strip, slots), out_shape...  97.2 us
    pallas_call x1, Pallas kernels, invert_call(): pl.pallas_call(functools.partial(invert, width), out_shape=(jax.ShapeDtyp...  18.2 us

profile of v5, /device:TPU:1, one launch (start us, length us, event | category | flops | bytes accessed | tf_op | source)
XLA Modules:
  0.0 116.7 jit_solution(5486633637222303595)
XLA Ops:
  1.3 97.2 %collect.1 = (f32[1792,1792]{1,0:T(8,128)S(1)}, f32[1,2]{1,0:T(1,128)S(1)}) custom-call(bf16[384,1728]{1,0:T(8,128)(2,1)} %bitcast.4, s32[1,48]{1,0:T(1,128)} %bitcast.5, f32[1]{0:T(128)S(6)} %copy.5.damping), custom_call_target="tpu_custom_call" | custom-call | tf_op jit(solution)/shard_map/collect/pallas_call | solution.py:414
  98.5 18.2 %invert.1 = (f32[432,1728]{1,0:T(8,128)}, f32[1,1]{1,0:T(1,128)}) custom-call(f32[1792,1792]{1,0:T(8,128)S(1)} %get-tuple-element.6.gram, f32[1,2]{1,0:T(1,128)S(1)} %get-tuple-element.7.stats), custom_call_target="tpu_custom_call" | custom-call | tf_op jit(solution)/shard_map/invert/pallas_call | solution.py:387
